TPU v7x, 512 devices: a whole 4x4x16 slice. The times are simulated.
512 devices in a mesh: mem: 16 (over x_lo, y, core), tile: 32 (over x_hi, z).
Axes of the slice: x: 4 (x_hi: 2, x_lo: 2; x = x_hi * 2 + x_lo), y: 4, z: 16, core: 2. Of those that a mesh axis runs over, the one named last changes fastest.
Arguments:
- perturbations: bfloat16 [32, 16, 512, 512], P('mem', None, 'tile'), may hold values from -6 to 6
- control: float32 [32, 16, 512, 512], P('mem', None, 'tile'), may hold values from -6 to 6
- innovation: float32 [16, 512, 512], P(None, 'tile'), may hold values from -6 to 6
- precision_field: float32 [16, 512, 512], P(None, 'tile'), may hold values from 0.2 to 5
- smooth_kernel: float32 [5, 5], replicated, may hold values from 0.2 to 1
- vertical_loc: float32 [16, 16], replicated, may hold values from -1.5 to 1.5
Outputs:
- increment: float32 [16, 512, 512], P(None, 'tile')
- gradient: float32 [32, 16, 512, 512], P('mem', None, 'tile')
All inputs are finite; a program needn't handle non-finite values.
Results may differ from a plain program's by a relative error of at most 0.0003.
Values sent between devices are 32-bit elements; how exact they have to be, the bound alone decides.
A program may use at most 64 MiB of HBM per device.

v0:
```python
import jax
import jax.numpy as jnp
from jax import lax
from jax.sharding import PartitionSpec as P


def extended_2(cells, sides, width):
    for axis, dim in sides:
        count = lax.axis_size(axis)
        head = lax.slice_in_dim(cells, 0, width, axis=dim)
        tail = lax.slice_in_dim(cells, cells.shape[dim] - width, cells.shape[dim], axis=dim)
        cells = jnp.concatenate(
            [
                lax.ppermute(tail, axis, [(i, (i + 1) % count) for i in range(count)]),
                cells,
                lax.ppermute(head, axis, [((i + 1) % count, i) for i in range(count)]),
            ],
            axis=dim,
        )
    return cells


def stencil_step(extended, weights):
    width = extended.shape[2] - 4
    rows = extended.shape[3]
    zeros_pad = jnp.zeros(extended.shape[:3] + (2,), jnp.float32)
    padded = jnp.concatenate([zeros_pad, extended, zeros_pad], axis=3)
    total = jnp.zeros(extended.shape[:2] + (width, rows), jnp.float32)
    for a in range(5):
        for b in range(5):
            total = total + weights[a, b] * padded[:, :, a : a + width, b : b + rows]
    return total


def forward_smooth(field, weights):
    current = field
    for step in range(4):
        extended = extended_2(current, (("tile", 2),), 2)
        current = stencil_step(extended, weights)
    return current


def adjoint_smooth(field, weights):
    current = field
    for step in range(4):
        extended = extended_2(current, (("tile", 2),), 2)
        current = stencil_step(extended, weights)
    return current


def local(perturbations, control, innovation, precision_field, smooth_kernel, vertical_loc):
    weights = smooth_kernel / jnp.sum(smooth_kernel)
    flipped = weights[::-1, ::-1]
    mixed = jnp.einsum("lm,kmij->klij", vertical_loc, control, precision=lax.Precision.HIGHEST)
    localized = forward_smooth(mixed, weights)
    pert_float = perturbations.astype(jnp.float32)
    contribution = jnp.sum(pert_float * localized, axis=0)
    increment = lax.psum(contribution, "mem")
    weighted = precision_field * (increment - innovation)
    adjoint_in = pert_float * weighted[None]
    smoothed_back = adjoint_smooth(adjoint_in, flipped)
    gradient = control + jnp.einsum(
        "ml,kmij->klij", vertical_loc, smoothed_back, precision=lax.Precision.HIGHEST
    )
    return (increment, gradient)


def solution(mesh):
    in_specs = (
        P("mem", None, "tile", None),
        P("mem", None, "tile", None),
        P(None, "tile", None),
        P(None, "tile", None),
        P(),
        P(),
    )
    out_specs = (P(None, "tile", None), P("mem", None, "tile", None))
    return jax.shard_map(local, mesh=mesh, in_specs=in_specs, out_specs=out_specs, check_vma=False)
```

profile of v0, /device:TPU:1, one launch (start us, length us, event | category | flops | bytes accessed | tf_op | source)
XLA Modules:
  0.0 425.7 jit_solution(8905926990211255650)
XLA Ops:
  7.9 2.8 convolution_bitcast_fusion.1
  10.7 4.4 %collective-permute-start = (f32[2,16,2,512]{3,1,2,0:T(8,128)S(1)}, f32[2,16,2,512]{3,1,2,0:T(8,128)S(1)}, u32[]{:S(2)}, u32[]{:S(2)}) collective-permute-start(f32[2,16,2,512]{3,1,2,0:T(8,128)S(1)} %get-tuple-element.20), channel_id=1, source_target_pairs={{0,1},{1,2},{2,3},{3,4},{4,5},{5,6},{6,7},{7,8},{8,9},{9,10},{10,1... | collective-permute-start | bytes 393224 | tf_op jit(solution)/shard_map/ppermute | solution.py:14
  15.1 12.0 %collective-permute-start.1 = (f32[2,16,2,512]{3,1,2,0:T(8,128)S(1)}, f32[2,16,2,512]{3,1,2,0:T(8,128)S(1)}, u32[]{:S(2)}, u32[]{:S(2)}) collective-permute-start(f32[2,16,2,512]{3,1,2,0:T(8,128)S(1)} %get-tuple-element.21), channel_id=1, source_target_pairs={{1,0},{2,1},{3,2},{4,3},{5,4},{6,5},{7,6},{8,7},{9,8},{10,9},{11,1... | collective-permute-start | bytes 393224 | tf_op jit(solution)/shard_map/ppermute | solution.py:16
  29.9 21.1 %fusion.201 = f32[2,16,16,512]{3,1,2,0:T(8,128)S(1)} fusion(f32[2,16,16,512]{3,1,2,0:T(8,128)S(1)} %convolution_bitcast_fusion.1, f32[2,16,2,512]{3,1,2,0:T(8,128)S(1)} %collective-permute-done.1, f32[2,16,2,512]{3,1,2,0:T(8,128)S(1)} %collective-permute-done, f32[2,16,20,512]{3,1,2,0:T(8,128)S(1)} %pad_maximum_fusion, f32[]{:T(128)} %bitcast.27, ...), kind=kLoop, calls=%fused_computation.403 | loop fusion | flops 13893632 | bytes 3670116 | tf_op jit(solution)/shard_map/add | solution.py:31
  51.0 1.9 collective-permute-start.2
  52.9 7.1 %collective-permute-start.3 = (f32[2,16,2,512]{3,1,2,0:T(8,128)S(1)}, f32[2,16,2,512]{3,1,2,0:T(8,128)S(1)}, u32[]{:S(2)}, u32[]{:S(2)}) collective-permute-start(f32[2,16,2,512]{3,1,2,0:T(8,128)S(1)} %get-tuple-element.19), channel_id=1, source_target_pairs={{1,0},{2,1},{3,2},{4,3},{5,4},{6,5},{7,6},{8,7},{9,8},{10,9},{11,1... | collective-permute-start | bytes 393224 | tf_op jit(solution)/shard_map/ppermute | solution.py:16
  62.2 21.2 %fusion.174 = f32[2,16,16,512]{3,1,2,0:T(8,128)S(1)} fusion(f32[2,16,16,512]{3,1,2,0:T(8,128)S(1)} %fusion.201, f32[2,16,2,512]{3,1,2,0:T(8,128)S(1)} %collective-permute-done.3, f32[2,16,2,512]{3,1,2,0:T(8,128)S(1)} %collective-permute-done.2, f32[2,16,20,512]{3,1,2,0:T(8,128)S(1)} %pad_maximum_fusion.1, f32[]{:T(128)} %bitcast.27, f32[]{:T(128)} %bitcast.26, ...), kind=kLoop, calls=%fused_computation.376 | loop fusion | flops 13893632 | bytes 3670116 | tf_op jit(solution)/shard_map/add | solution.py:31
  83.3 1.9 collective-permute-start.4
  85.3 7.4 %collective-permute-start.5 = (f32[2,16,2,512]{3,1,2,0:T(8,128)S(1)}, f32[2,16,2,512]{3,1,2,0:T(8,128)S(1)}, u32[]{:S(2)}, u32[]{:S(2)}) collective-permute-start(f32[2,16,2,512]{3,1,2,0:T(8,128)S(1)} %get-tuple-element.17), channel_id=1, source_target_pairs={{1,0},{2,1},{3,2},{4,3},{5,4},{6,5},{7,6},{8,7},{9,8},{10,9},{11,1... | collective-permute-start | bytes 393224 | tf_op jit(solution)/shard_map/ppermute | solution.py:16
  94.8 21.2 %fusion.147 = f32[2,16,16,512]{3,1,2,0:T(8,128)S(1)} fusion(f32[2,16,16,512]{3,1,2,0:T(8,128)S(1)} %fusion.174, f32[2,16,2,512]{3,1,2,0:T(8,128)S(1)} %collective-permute-done.5, f32[2,16,2,512]{3,1,2,0:T(8,128)S(1)} %collective-permute-done.4, f32[2,16,20,512]{3,1,2,0:T(8,128)S(1)} %pad_maximum_fusion.2, f32[]{:T(128)} %bitcast.27, f32[]{:T(128)} %bitcast.26, ...), kind=kLoop, calls=%fused_computation.349 | loop fusion | flops 13893632 | bytes 3670116 | tf_op jit(solution)/shard_map/add | solution.py:31
  117.9 7.7 %collective-permute-start.7 = (f32[2,16,2,512]{3,1,2,0:T(8,128)S(1)}, f32[2,16,2,512]{3,1,2,0:T(8,128)S(1)}, u32[]{:S(2)}, u32[]{:S(2)}) collective-permute-start(f32[2,16,2,512]{3,1,2,0:T(8,128)S(1)} %get-tuple-element.15), channel_id=1, source_target_pairs={{1,0},{2,1},{3,2},{4,3},{5,4},{6,5},{7,6},{8,7},{9,8},{10,9},{11,1... | collective-permute-start | bytes 393224 | tf_op jit(solution)/shard_map/ppermute | solution.py:16
  127.5 22.2 %fusion.428 = f32[16,16,512]{2,0,1:T(8,128)} fusion(f32[2,16,20,512]{3,1,2,0:T(8,128)S(1)} %pad_maximum_fusion.3, f32[2,16,2,512]{3,1,2,0:T(8,128)S(1)} %collective-permute-done.7, f32[2,16,16,512]{3,1,2,0:T(8,128)S(1)} %fusion.147, f32[2,16,2,512]{3,1,2,0:T(8,128)S(1)} %collective-permute-done.6, f32[]{:T(128)} %bitcast.27, f32[]{:T(128)} %bitcast.26, ...), kind=kLoop, calls=%fused_computation.624 | loop fusion | flops 14548992 | bytes 3670116 | tf_op jit(solution)/shard_map/reduce_sum | solution.py:57
  149.7 131.4 %all-reduce.18.cloned.1.call-done = f32[16,16,512]{2,0,1:T(8,128)} async-done(((f32[16,16,512]{2,0,1:T(8,128)}), f32[16,16,512]{2,0,1:T(8,128)}) %all-reduce.18.cloned.1.call-update) | async-done | bytes 524304 | tf_op jit(solution)/shard_map/psum | solution.py:58
  283.2 3.2 collective-permute-start.8
  286.4 6.5 %collective-permute-start.9 = (f32[2,16,2,512]{3,1,2,0:T(8,128)S(1)}, f32[2,16,2,512]{3,1,2,0:T(8,128)S(1)}, u32[]{:S(2)}, u32[]{:S(2)}) collective-permute-start(f32[2,16,2,512]{3,1,2,0:T(8,128)S(1)} %get-tuple-element.13), channel_id=1, source_target_pairs={{1,0},{2,1},{3,2},{4,3},{5,4},{6,5},{7,6},{8,7},{9,8},{10,9},{11,1... | collective-permute-start | bytes 393224 | tf_op jit(solution)/shard_map/ppermute | solution.py:16
  295.0 21.4 %fusion.93 = f32[2,16,16,512]{3,1,2,0:T(8,128)S(1)} fusion(f32[2,16,16,512]{3,1,2,0:T(8,128)S(1)} %convert_multiply_fusion, f32[2,16,2,512]{3,1,2,0:T(8,128)S(1)} %collective-permute-done.9, f32[2,16,2,512]{3,1,2,0:T(8,128)S(1)} %collective-permute-done.8, f32[2,16,20,512]{3,1,2,0:T(8,128)S(1)} %pad_maximum_fusion.4, f32[]{:T(128)} %bitcast.52, ...), kind=kLoop, calls=%fused_computation.295 | loop fusion | flops 13893632 | bytes 3670116 | tf_op jit(solution)/shard_map/add | solution.py:31
  318.4 7.8 %collective-permute-start.11 = (f32[2,16,2,512]{3,1,2,0:T(8,128)S(1)}, f32[2,16,2,512]{3,1,2,0:T(8,128)S(1)}, u32[]{:S(2)}, u32[]{:S(2)}) collective-permute-start(f32[2,16,2,512]{3,1,2,0:T(8,128)S(1)} %get-tuple-element.11), channel_id=1, source_target_pairs={{1,0},{2,1},{3,2},{4,3},{5,4},{6,5},{7,6},{8,7},{9,8},{10,9},{11,1... | collective-permute-start | bytes 393224 | tf_op jit(solution)/shard_map/ppermute | solution.py:16
  328.3 21.4 %fusion.66 = f32[2,16,16,512]{3,1,2,0:T(8,128)S(1)} fusion(f32[2,16,16,512]{3,1,2,0:T(8,128)S(1)} %fusion.93, f32[2,16,2,512]{3,1,2,0:T(8,128)S(1)} %collective-permute-done.11, f32[2,16,2,512]{3,1,2,0:T(8,128)S(1)} %collective-permute-done.10, f32[2,16,20,512]{3,1,2,0:T(8,128)S(1)} %pad_maximum_fusion.5, f32[]{:T(128)} %bitcast.52, f32[]{:T(128)} %bitcast.51, ...), kind=kLoop, calls=%fused_computation.268 | loop fusion | flops 13893632 | bytes 3670116 | tf_op jit(solution)/shard_map/add | solution.py:31
  349.7 1.9 collective-permute-start.12
  351.7 7.6 %collective-permute-start.13 = (f32[2,16,2,512]{3,1,2,0:T(8,128)S(1)}, f32[2,16,2,512]{3,1,2,0:T(8,128)S(1)}, u32[]{:S(2)}, u32[]{:S(2)}) collective-permute-start(f32[2,16,2,512]{3,1,2,0:T(8,128)S(1)} %get-tuple-element.9), channel_id=1, source_target_pairs={{1,0},{2,1},{3,2},{4,3},{5,4},{6,5},{7,6},{8,7},{9,8},{10,9},{11,1... | collective-permute-start | bytes 393224 | tf_op jit(solution)/shard_map/ppermute | solution.py:16
  361.1 21.5 %fusion.39 = f32[2,16,16,512]{3,1,2,0:T(8,128)S(1)} fusion(f32[2,16,16,512]{3,1,2,0:T(8,128)S(1)} %fusion.66, f32[2,16,2,512]{3,1,2,0:T(8,128)S(1)} %collective-permute-done.13, f32[2,16,2,512]{3,1,2,0:T(8,128)S(1)} %collective-permute-done.12, f32[2,16,20,512]{3,1,2,0:T(8,128)S(1)} %pad_maximum_fusion.6, f32[]{:T(128)} %bitcast.52, f32[]{:T(128)} %bitcast.51, ...), kind=kLoop, calls=%fused_computation.241 | loop fusion | flops 13893632 | bytes 3670116 | tf_op jit(solution)/shard_map/add | solution.py:31
  382.6 1.9 collective-permute-start.14
  384.6 7.4 %collective-permute-start.15 = (f32[2,16,2,512]{3,1,2,0:T(8,128)S(1)}, f32[2,16,2,512]{3,1,2,0:T(8,128)S(1)}, u32[]{:S(2)}, u32[]{:S(2)}) collective-permute-start(f32[2,16,2,512]{3,1,2,0:T(8,128)S(1)} %get-tuple-element.7), channel_id=1, source_target_pairs={{1,0},{2,1},{3,2},{4,3},{5,4},{6,5},{7,6},{8,7},{9,8},{10,9},{11,1... | collective-permute-start | bytes 393224 | tf_op jit(solution)/shard_map/ppermute | solution.py:16
  394.3 23.0 %fusion = f32[2,16,16,512]{3,1,2,0:T(8,128)S(1)} fusion(f32[2,16,16,512]{3,1,2,0:T(8,128)S(1)} %fusion.39, f32[2,16,2,512]{3,1,2,0:T(8,128)S(1)} %collective-permute-done.15, f32[2,16,2,512]{3,1,2,0:T(8,128)S(1)} %collective-permute-done.14, f32[2,16,20,512]{3,1,2,0:T(8,128)S(1)} %pad_maximum_fusion.7, f32[2,16,16,512]{3,2,1,0:T(8,128)S(1)} %copy-done.3, ...), kind=kOutput, calls=%fused_computation.161 | convolution fusion | flops 64487424 | bytes 4719716 | tf_op jit(solution)/shard_map/ml,kmij->klij/dot_general | solution.py:62
  (61 shorter events, 25.5 us)
Async XLA Ops:
  7.2 0.7 copy-start
  7.2 19.8 %copy-start.6 = (f32[5,5]{1,0:T(8,128)S(1)}, f32[5,5]{1,0:T(8,128)}, u32[]{:S(2)}) copy-start(f32[5,5]{1,0:T(8,128)} %param.10) | copy-start | bytes 304
  7.2 273.9 %all-reduce.18.cloned.1.call-start = ((), (), s32[]{:S(2)}) async-start(), calls=%async_computation | async-start | bytes 1048576 | tf_op jit(solution)/shard_map/psum | solution.py:58
  10.7 19.1 %collective-permute-start = (f32[2,16,2,512]{3,1,2,0:T(8,128)S(1)}, f32[2,16,2,512]{3,1,2,0:T(8,128)S(1)}, u32[]{:S(2)}, u32[]{:S(2)}) collective-permute-start(f32[2,16,2,512]{3,1,2,0:T(8,128)S(1)} %get-tuple-element.20), channel_id=1, source_target_pairs={{0,1},{1,2},{2,3},{3,4},{4,5},{5,6},{6,7},{7,8},{8,9},{9,10},{10,1... | collective-permute-start | bytes 393224 | tf_op jit(solution)/shard_map/ppermute | solution.py:14
  15.1 14.7 %collective-permute-start.1 = (f32[2,16,2,512]{3,1,2,0:T(8,128)S(1)}, f32[2,16,2,512]{3,1,2,0:T(8,128)S(1)}, u32[]{:S(2)}, u32[]{:S(2)}) collective-permute-start(f32[2,16,2,512]{3,1,2,0:T(8,128)S(1)} %get-tuple-element.21), channel_id=1, source_target_pairs={{1,0},{2,1},{3,2},{4,3},{5,4},{6,5},{7,6},{8,7},{9,8},{10,9},{11,1... | collective-permute-start | bytes 393224 | tf_op jit(solution)/shard_map/ppermute | solution.py:16
  51.0 9.5 %collective-permute-start.2 = (f32[2,16,2,512]{3,1,2,0:T(8,128)S(1)}, f32[2,16,2,512]{3,1,2,0:T(8,128)S(1)}, u32[]{:S(2)}, u32[]{:S(2)}) collective-permute-start(f32[2,16,2,512]{3,1,2,0:T(8,128)S(1)} %get-tuple-element.18), channel_id=1, source_target_pairs={{0,1},{1,2},{2,3},{3,4},{4,5},{5,6},{6,7},{7,8},{8,9},{9,10},{10,1... | collective-permute-start | bytes 393224 | tf_op jit(solution)/shard_map/ppermute | solution.py:14
  52.9 9.0 %collective-permute-start.3 = (f32[2,16,2,512]{3,1,2,0:T(8,128)S(1)}, f32[2,16,2,512]{3,1,2,0:T(8,128)S(1)}, u32[]{:S(2)}, u32[]{:S(2)}) collective-permute-start(f32[2,16,2,512]{3,1,2,0:T(8,128)S(1)} %get-tuple-element.19), channel_id=1, source_target_pairs={{1,0},{2,1},{3,2},{4,3},{5,4},{6,5},{7,6},{8,7},{9,8},{10,9},{11,1... | collective-permute-start | bytes 393224 | tf_op jit(solution)/shard_map/ppermute | solution.py:16
  83.3 9.7 %collective-permute-start.4 = (f32[2,16,2,512]{3,1,2,0:T(8,128)S(1)}, f32[2,16,2,512]{3,1,2,0:T(8,128)S(1)}, u32[]{:S(2)}, u32[]{:S(2)}) collective-permute-start(f32[2,16,2,512]{3,1,2,0:T(8,128)S(1)} %get-tuple-element.16), channel_id=1, source_target_pairs={{0,1},{1,2},{2,3},{3,4},{4,5},{5,6},{6,7},{7,8},{8,9},{9,10},{10,1... | collective-permute-start | bytes 393224 | tf_op jit(solution)/shard_map/ppermute | solution.py:14
  85.3 9.3 %collective-permute-start.5 = (f32[2,16,2,512]{3,1,2,0:T(8,128)S(1)}, f32[2,16,2,512]{3,1,2,0:T(8,128)S(1)}, u32[]{:S(2)}, u32[]{:S(2)}) collective-permute-start(f32[2,16,2,512]{3,1,2,0:T(8,128)S(1)} %get-tuple-element.17), channel_id=1, source_target_pairs={{1,0},{2,1},{3,2},{4,3},{5,4},{6,5},{7,6},{8,7},{9,8},{10,9},{11,1... | collective-permute-start | bytes 393224 | tf_op jit(solution)/shard_map/ppermute | solution.py:16
  116.0 9.7 %collective-permute-start.6 = (f32[2,16,2,512]{3,1,2,0:T(8,128)S(1)}, f32[2,16,2,512]{3,1,2,0:T(8,128)S(1)}, u32[]{:S(2)}, u32[]{:S(2)}) collective-permute-start(f32[2,16,2,512]{3,1,2,0:T(8,128)S(1)} %get-tuple-element.14), channel_id=1, source_target_pairs={{0,1},{1,2},{2,3},{3,4},{4,5},{5,6},{6,7},{7,8},{8,9},{9,10},{10,1... | collective-permute-start | bytes 393224 | tf_op jit(solution)/shard_map/ppermute | solution.py:14
  117.9 9.6 %copy-start.1 = (bf16[2,16,16,512]{3,2,1,0:T(8,128)(2,1)S(1)}, bf16[2,16,16,512]{3,2,1,0:T(8,128)(2,1)}, u32[]{:S(2)}) copy-start(bf16[2,16,16,512]{3,2,1,0:T(8,128)(2,1)} %param.6) | copy-start | bytes 1572868
  117.9 9.5 %collective-permute-start.7 = (f32[2,16,2,512]{3,1,2,0:T(8,128)S(1)}, f32[2,16,2,512]{3,1,2,0:T(8,128)S(1)}, u32[]{:S(2)}, u32[]{:S(2)}) collective-permute-start(f32[2,16,2,512]{3,1,2,0:T(8,128)S(1)} %get-tuple-element.15), channel_id=1, source_target_pairs={{1,0},{2,1},{3,2},{4,3},{5,4},{6,5},{7,6},{8,7},{9,8},{10,9},{11,1... | collective-permute-start | bytes 393224 | tf_op jit(solution)/shard_map/ppermute | solution.py:16
  127.5 153.6 %copy-start.4 = (f32[16,16,512]{2,1,0:T(8,128)S(1)}, f32[16,16,512]{2,1,0:T(8,128)}, u32[]{:S(2)}) copy-start(f32[16,16,512]{2,1,0:T(8,128)} %param.9) | copy-start | bytes 1572868
  127.5 153.6 %copy-start.5 = (f32[16,16,512]{2,1,0:T(8,128)S(1)}, f32[16,16,512]{2,1,0:T(8,128)}, u32[]{:S(2)}) copy-start(f32[16,16,512]{2,1,0:T(8,128)} %param.8) | copy-start | bytes 1572868
  283.2 11.1 %collective-permute-start.8 = (f32[2,16,2,512]{3,1,2,0:T(8,128)S(1)}, f32[2,16,2,512]{3,1,2,0:T(8,128)S(1)}, u32[]{:S(2)}, u32[]{:S(2)}) collective-permute-start(f32[2,16,2,512]{3,1,2,0:T(8,128)S(1)} %get-tuple-element.12), channel_id=1, source_target_pairs={{0,1},{1,2},{2,3},{3,4},{4,5},{5,6},{6,7},{7,8},{8,9},{9,10},{10,1... | collective-permute-start | bytes 393224 | tf_op jit(solution)/shard_map/ppermute | solution.py:14
  286.4 8.5 %collective-permute-start.9 = (f32[2,16,2,512]{3,1,2,0:T(8,128)S(1)}, f32[2,16,2,512]{3,1,2,0:T(8,128)S(1)}, u32[]{:S(2)}, u32[]{:S(2)}) collective-permute-start(f32[2,16,2,512]{3,1,2,0:T(8,128)S(1)} %get-tuple-element.13), channel_id=1, source_target_pairs={{1,0},{2,1},{3,2},{4,3},{5,4},{6,5},{7,6},{8,7},{9,8},{10,9},{11,1... | collective-permute-start | bytes 393224 | tf_op jit(solution)/shard_map/ppermute | solution.py:16
  316.4 10.2 %collective-permute-start.10 = (f32[2,16,2,512]{3,1,2,0:T(8,128)S(1)}, f32[2,16,2,512]{3,1,2,0:T(8,128)S(1)}, u32[]{:S(2)}, u32[]{:S(2)}) collective-permute-start(f32[2,16,2,512]{3,1,2,0:T(8,128)S(1)} %get-tuple-element.10), channel_id=1, source_target_pairs={{0,1},{1,2},{2,3},{3,4},{4,5},{5,6},{6,7},{7,8},{8,9},{9,10},{10,1... | collective-permute-start | bytes 393224 | tf_op jit(solution)/shard_map/ppermute | solution.py:14
  318.4 9.8 %collective-permute-start.11 = (f32[2,16,2,512]{3,1,2,0:T(8,128)S(1)}, f32[2,16,2,512]{3,1,2,0:T(8,128)S(1)}, u32[]{:S(2)}, u32[]{:S(2)}) collective-permute-start(f32[2,16,2,512]{3,1,2,0:T(8,128)S(1)} %get-tuple-element.11), channel_id=1, source_target_pairs={{1,0},{2,1},{3,2},{4,3},{5,4},{6,5},{7,6},{8,7},{9,8},{10,9},{11,1... | collective-permute-start | bytes 393224 | tf_op jit(solution)/shard_map/ppermute | solution.py:16
  349.7 9.7 %collective-permute-start.12 = (f32[2,16,2,512]{3,1,2,0:T(8,128)S(1)}, f32[2,16,2,512]{3,1,2,0:T(8,128)S(1)}, u32[]{:S(2)}, u32[]{:S(2)}) collective-permute-start(f32[2,16,2,512]{3,1,2,0:T(8,128)S(1)} %get-tuple-element.8), channel_id=1, source_target_pairs={{0,1},{1,2},{2,3},{3,4},{4,5},{5,6},{6,7},{7,8},{8,9},{9,10},{10,1... | collective-permute-start | bytes 393224 | tf_op jit(solution)/shard_map/ppermute | solution.py:14
  351.7 9.3 %collective-permute-start.13 = (f32[2,16,2,512]{3,1,2,0:T(8,128)S(1)}, f32[2,16,2,512]{3,1,2,0:T(8,128)S(1)}, u32[]{:S(2)}, u32[]{:S(2)}) collective-permute-start(f32[2,16,2,512]{3,1,2,0:T(8,128)S(1)} %get-tuple-element.9), channel_id=1, source_target_pairs={{1,0},{2,1},{3,2},{4,3},{5,4},{6,5},{7,6},{8,7},{9,8},{10,9},{11,1... | collective-permute-start | bytes 393224 | tf_op jit(solution)/shard_map/ppermute | solution.py:16
  361.1 30.8 %copy-start.2 = (f32[16,16,512]{2,0,1:T(8,128)S(1)}, f32[16,16,512]{2,0,1:T(8,128)}, u32[]{:S(2)}) copy-start(f32[16,16,512]{2,0,1:T(8,128)} %all-reduce.18.cloned.1.call-done) | copy-start | bytes 1572868
  382.6 10.4 %collective-permute-start.14 = (f32[2,16,2,512]{3,1,2,0:T(8,128)S(1)}, f32[2,16,2,512]{3,1,2,0:T(8,128)S(1)}, u32[]{:S(2)}, u32[]{:S(2)}) collective-permute-start(f32[2,16,2,512]{3,1,2,0:T(8,128)S(1)} %get-tuple-element.6), channel_id=1, source_target_pairs={{0,1},{1,2},{2,3},{3,4},{4,5},{5,6},{6,7},{7,8},{8,9},{9,10},{10,1... | collective-permute-start | bytes 393224 | tf_op jit(solution)/shard_map/ppermute | solution.py:14
  384.6 9.3 %collective-permute-start.15 = (f32[2,16,2,512]{3,1,2,0:T(8,128)S(1)}, f32[2,16,2,512]{3,1,2,0:T(8,128)S(1)}, u32[]{:S(2)}, u32[]{:S(2)}) collective-permute-start(f32[2,16,2,512]{3,1,2,0:T(8,128)S(1)} %get-tuple-element.7), channel_id=1, source_target_pairs={{1,0},{2,1},{3,2},{4,3},{5,4},{6,5},{7,6},{8,7},{9,8},{10,9},{11,1... | collective-permute-start | bytes 393224 | tf_op jit(solution)/shard_map/ppermute | solution.py:16
  393.1 1.2 copy-start.3
Sparse Core Ops, SparseCore 0:
  149.9 131.2 all-reduce.17
where the time goes:
time: 430 us; the launch traced here: 426 us
  other arithmetic  154 us (36%)
  waiting for transfers between devices  142 us (33%)
  starting transfers between devices  82.7 us (19%)
  matrix products  25.8 us (6%)
  between operations  14.5 us (3%)
  local copies, waits for them, and re-layouts  6.58 us (2%)
    psum x1, waiting for transfers between devices, local(): increment = lax.psum(contribution, 'mem')  131 us
    add x6, other arithmetic, stencil_step(): total = total + weights[a, b] * padded[:, :, a:a + width, b:b + rows]  128 us
    ppermute x8, starting transfers between devices, extended_2(): lax.ppermute(head, axis, [((i + 1) % count, i) for i in range(count)])  63.5 us
    dot_general x1, matrix products, local(): jnp.einsum('ml,kmij->klij', vertical_loc, smoothed_back, precision=lax.Pr...  23 us
    reduce_sum x1, other arithmetic, local(): contribution = jnp.sum(pert_float * localized, axis=0)  22.2 us
    ppermute x8, starting transfers between devices, extended_2(): lax.ppermute(tail, axis, [(i, (i + 1) % count) for i in range(count)])  19.1 us
    ppermute x8, waiting for transfers between devices, extended_2(): lax.ppermute(head, axis, [((i + 1) % count, i) for i in range(count)])  9.05 us
  transfers between devices with their start and end apart: 17, of which 13 were waited for; matrix products, arithmetic and copies ran while one was open for 1% of the time, Pallas kernels for 0%

commit v1 on v0

v1 whole, which is shorter than its diff:
```python
import functools

import jax
import jax.numpy as jnp
from jax import lax
from jax.experimental import pallas as pl
from jax.experimental.pallas import tpu as pltpu
from jax.sharding import PartitionSpec as P

MESH = pl.DeviceIdType.MESH
HIGHEST = lax.Precision.HIGHEST
F32 = jnp.float32
BF16 = jnp.bfloat16


def lanes_of(shape):
    return lax.broadcasted_iota(jnp.int32, shape, len(shape) - 1)


def rows_of(shape):
    return lax.broadcasted_iota(jnp.int32, shape, len(shape) - 2)


def roll(x, shift):
    return pltpu.roll(x, shift % x.shape[-1], x.ndim - 1)


def composed_rows(sk, flip, variant):
    shape = (16, 1024)
    lane = lanes_of(shape)
    col = lane % 32
    start = jnp.where(lane == 264 + rows_of(shape), 1.0, 0.0).astype(F32)
    if variant == 0:
        inside = col >= 8
    elif variant == 2:
        inside = col < 24
    else:
        inside = None

    def tap(a, b):
        return sk[4 - a, 4 - b] if flip else sk[a, b]

    def one_pass(step, r):
        moved = [roll(r, 32 * (a - 2)) if a != 2 else r for a in range(5)]
        out = None
        for b in range(5):
            part = moved[0] * tap(0, b)
            for a in range(1, 5):
                part = part + moved[a] * tap(a, b)
            part = roll(part, b - 2) if b != 2 else part
            out = part if out is None else out + part
        if inside is not None:
            out = jnp.where(inside, out, 0.0)
        return out

    r = lax.fori_loop(0, 4, one_pass, start)
    total = sk[0, 0]
    for n in range(1, 25):
        total = total + sk[n // 5, n % 5]
    total = jnp.full((16, 1024), total, F32)
    square = total * total
    return r / (square * square)


def split(x):
    hi = x.astype(BF16)
    lo = (x - hi.astype(F32)).astype(BF16)
    return hi, lo


def kernel(
    ctl_h, pert_h, innov_h, prec_h, sk, vloc,
    inc_h, grad_h,
    ctl_v, pert_v, pert_f, innov_v, prec_v, xc, pt, xb, w_own, w_left, w_right, field,
    contrib, core_in, chip_sum, parts_in, inc_all, halo_w, own_w, prec_p, innov_p, grad_v, inc_v,
    in_sem, out_sem, c_send, c_recv, p_send, p_recv, k_send, k_recv, r_send, r_recv,
    a_send, a_recv, h_send, h_recv, f_send, f_recv, g_send, g_recv,
):
    m = lax.axis_index("mem")
    t = lax.axis_index("tile")
    tiles = lax.axis_size("tile")
    right = lax.rem(t + 1, tiles)
    left = lax.rem(t + tiles - 1, tiles)
    chip = m // 2
    core = m % 2
    sibling = 2 * chip + 1 - core

    loads = [
        [
            pltpu.make_async_copy(src.at[:, pl.ds(128 * q, 128)], dst.at[q], in_sem.at[n, q])
            for q in range(4)
        ]
        for n, (src, dst) in enumerate(
            [(ctl_h, ctl_v), (pert_h, pert_v), (innov_h, innov_v), (prec_h, prec_v)]
        )
    ]
    for load in loads:
        for copy in load:
            copy.start()

    def arrive(n):
        for copy in loads[n]:
            copy.wait()

    def peer(d):
        other = jnp.bitwise_xor(chip, d)
        return other, 2 * other + core

    barrier = pltpu.get_barrier_semaphore()

    def greet(mem, tile):
        pl.semaphore_signal(barrier, inc=1, device_id=(mem, tile), device_id_type=MESH)

    greet(sibling, t)
    for d in range(1, 8):
        greet(peer(d)[1], t)
    for k in range(4):
        greet(2 * k + core, right)
        greet(2 * (k + 4) + core, left)
    greet(m, jnp.where(chip < 4, left, right))

    col16 = lanes_of((128, 16))
    row128 = rows_of((128, 16))
    pick = jnp.where(row128 % 16 == col16, 1.0, 0.0).astype(F32)
    wide = jnp.dot(pick, vloc[...], precision=HIGHEST, preferred_element_type=F32)
    lane16 = lanes_of((16, 128))
    spread = jnp.where(lane16 % 16 == rows_of((16, 128)), 1.0, 0.0).astype(F32)
    full = jnp.dot(wide, spread, precision=HIGHEST, preferred_element_type=F32)
    same = rows_of((128, 128)) // 16 == lanes_of((128, 128)) // 16
    mix = jnp.where(same, full, 0.0)
    mix_t = mix.T

    def columns(ref, i, count):
        return [ref[q, pl.ds(i, count, stride=16), :] for q in range(4)]

    def remote(src, dst, send, recv, mem, tile):
        return pltpu.make_async_remote_copy(
            src_ref=src, dst_ref=dst, send_sem=send, recv_sem=recv,
            device_id=(mem, tile), device_id_type=MESH,
        )

    arrive(0)
    c_copies = []
    for n, group in enumerate([range(8, 12), range(0, 4), range(12, 16), range(4, 8)]):
        for i in group:
            x = jnp.concatenate(columns(ctl_v, i, 32), axis=0)
            x = jnp.dot(mix, x, precision=HIGHEST, preferred_element_type=F32)
            xc[8 + i] = x.T
        if n == 0:
            pl.semaphore_wait(barrier, 17)
        first = group[0]
        to_right = first >= 8
        target = first - 8 if to_right else 24 + first
        copy = remote(
            xc.at[pl.ds(8 + first, 4)], xc.at[pl.ds(target, 4)],
            c_send.at[n], c_recv.at[n], m, right if to_right else left,
        )
        copy.start()
        c_copies.append(copy)

    lane8 = lanes_of((8, 128))

    def prepare(index, x):
        top = jnp.where(lane8 >= 32, roll(x[120:128], 32), 0.0)
        bottom = jnp.where(lane8 < 96, roll(x[0:8], -32), 0.0)
        hi, lo = split(jnp.concatenate([top, x, bottom], axis=0))
        xb[index, :, 0:128] = hi
        xb[index, :, 128:256] = lo

    def each(first, last, body):
        def step(i, carry):
            body(i)
            return carry

        lax.fori_loop(first, last, step, 0)

    each(8, 24, lambda i: prepare(i, xc[i]))

    def build(direction):
        for variant in range(3):
            base = composed_rows(sk, direction == 1, variant)
            for i in range(16):
                hi, lo = split(roll(base, 32 * i) if i else base)
                at = 16 * i
                w_own[direction, variant, at : at + 16, :] = hi[:, 256:768]
                w_own[direction, variant, 256 + at : 272 + at, :] = lo[:, 256:768]
                if i < 8:
                    w_left[direction, variant, at : at + 16, :] = hi[:, 0:256]
                    w_left[direction, variant, 128 + at : 144 + at, :] = lo[:, 0:256]
                else:
                    w_right[direction, variant, at - 128 : at - 112, :] = hi[:, 768:1024]
                    w_right[direction, variant, at : at + 16, :] = lo[:, 768:1024]

    build(0)

    lane3 = lanes_of((1, 1, 128))

    def block(w, lons, rows):
        first, last = lons
        rhs = xb[first:last, rows, :].reshape((last - first) * 32, 256)
        out = jnp.dot(w[...], rhs, preferred_element_type=F32)
        half = out.shape[0] // 2
        out = out[:half, :128] + out[:half, 128:] + out[half:, :128]
        return out.reshape(half // 16, 16, 128)

    def smooth(weights, direction, lons, put):
        def at(variant, b):
            rows = pl.ds(pl.multiple_of(16 * b, 16), 32)
            return block(weights.at[direction, variant], lons, rows)

        each(1, 7, lambda b: put(pl.ds(pl.multiple_of(16 * b, 16), 16), at(1, b)))
        put(pl.ds(0, 16), jnp.where(lane3 < 32, at(0, 0), at(1, 0)))
        put(pl.ds(112, 16), jnp.where(lane3 >= 96, at(2, 7), at(1, 7)))

    def put_own(rows, value):
        field[:, rows, :] = value

    def add_left(rows, value):
        field[0:8, rows, :] = field[0:8, rows, :] + value

    def add_right(rows, value):
        field[8:16, rows, :] = field[8:16, rows, :] + value

    smooth(w_own, 0, (8, 24), put_own)

    arrive(1)
    pert_f[...] = pert_v[...].astype(F32)
    for i in range(16):
        pt[8 + i] = jnp.concatenate(columns(pert_f, i, 32), axis=0).T

    first_half = lanes_of((64, 128)) % 32 < 16

    def packed(ref, i):
        parts = [p for p in columns(ref, i, 16) for _ in range(2)]
        x = jnp.concatenate(parts, axis=0).T
        return jnp.where(first_half, x[0:64], x[64:128])

    arrive(2)
    arrive(3)
    for i in range(16):
        innov_p[i] = packed(innov_v, i)
        prec_p[i] = packed(prec_v, i)

    build(1)

    for copy in c_copies:
        copy.wait()
    p_copies = [
        remote(pt.at[pl.ds(16, 8)], pt.at[pl.ds(0, 8)], p_send.at[0], p_recv.at[0], m, right),
        remote(pt.at[pl.ds(8, 8)], pt.at[pl.ds(24, 8)], p_send.at[1], p_recv.at[1], m, left),
    ]
    for copy in p_copies:
        copy.start()
    each(0, 8, lambda i: prepare(i, xc[i]))
    each(24, 32, lambda i: prepare(i, xc[i]))
    smooth(w_left, 0, (0, 8), add_left)
    smooth(w_right, 0, (24, 32), add_right)

    for i in range(16):
        x = pt[8 + i] * field[i]
        top, bottom = x[0:64], x[64:128]
        here = jnp.where(first_half, top, bottom)
        there = jnp.where(first_half, roll(top, -16), roll(bottom, 16))
        contrib[i % 2, i // 2] = here + there

    copy = remote(contrib.at[1 - core], core_in, k_send.at[0], k_recv.at[0], sibling, t)
    copy.start()
    copy.wait()
    chip_sum[...] = contrib[core] + core_in[...]
    copies = []
    for d in range(1, 8):
        other, mem = peer(d)
        copy = remote(chip_sum.at[other], parts_in.at[chip], r_send.at[d], r_recv.at[d], mem, t)
        copy.start()
        copies.append(copy)
    for copy in copies:
        copy.wait()
    total = chip_sum[chip]
    for d in range(1, 8):
        total = total + parts_in[peer(d)[0]]

    inc_all[m] = total
    own_w[...] = prec_p[m] * (total - innov_p[m])
    a_copies = []
    for d in range(1, 8):
        other, mem = peer(d)
        copy = remote(inc_all.at[m], inc_all.at[m], a_send.at[d], a_recv.at[d], mem, t)
        copy.start()
        a_copies.append(copy)
    beside = jnp.where(chip < 4, left, right)
    slot = lax.rem(m + 8, 16)
    h_copies = []
    for d in range(8):
        other, mem = peer(d)
        copy = remote(own_w, halo_w.at[slot], h_send.at[d], h_recv.at[chip], mem, beside)
        copy.start()
        h_copies.append(copy)

    f_copies = []
    for d in range(8):
        other, mem = peer(d)
        if d:
            a_copies[d - 1].wait()
        copy = remote(inc_all.at[mem], inc_all.at[mem], f_send.at[d], f_recv.at[d], sibling, t)
        copy.start()
        f_copies.append(copy)
    g_copies = []
    for k in range(8):
        arrived = remote(own_w, halo_w.at[slot], h_send.at[k], h_recv.at[k], m, beside)
        arrived.wait_recv()
        at = lax.rem(2 * k + core + 8, 16)
        copy = remote(halo_w.at[at], halo_w.at[at], g_send.at[k], g_recv.at[k], sibling, t)
        copy.start()
        g_copies.append(copy)
    for copy in f_copies:
        copy.wait()

    def adjoint_input(i, w):
        top = jnp.where(first_half, w, roll(w, 16))
        bottom = jnp.where(first_half, roll(w, -16), w)
        prepare(i, pt[i] * jnp.concatenate([top, bottom], axis=0))

    each(0, 16, lambda i: adjoint_input(8 + i, prec_p[i] * (inc_all[i] - innov_p[i])))
    smooth(w_own, 1, (8, 24), put_own)

    for i in range(16):
        w = inc_all[i]
        top = jnp.where(first_half, w, roll(w, 16))
        bottom = jnp.where(first_half, roll(w, -16), w)
        x = jnp.concatenate([top, bottom], axis=0).T
        for q in range(4):
            inc_v[q, pl.ds(i, 16, stride=16), :] = x[32 * q : 32 * q + 16]
    stores = []

    def store(src, dst, n):
        for q in range(4):
            copy = pltpu.make_async_copy(src.at[q], dst.at[:, pl.ds(128 * q, 128)], out_sem.at[n, q])
            copy.start()
            stores.append(copy)

    store(inc_v, inc_h, 0)

    for copy in g_copies:
        copy.wait()
    for copy in h_copies:
        copy.wait_send()
    for copy in p_copies:
        copy.wait()
    each(0, 8, lambda i: adjoint_input(i, halo_w[i]))
    each(24, 32, lambda i: adjoint_input(i, halo_w[i - 16]))
    smooth(w_left, 1, (0, 8), add_left)
    smooth(w_right, 1, (24, 32), add_right)

    for i in range(16):
        x = jnp.dot(mix_t, field[i].T, precision=HIGHEST, preferred_element_type=F32)
        x = x + jnp.concatenate(columns(ctl_v, i, 32), axis=0)
        for q in range(4):
            grad_v[q, pl.ds(i, 32, stride=16), :] = x[32 * q : 32 * q + 32]
    store(grad_v, grad_h, 1)
    for copy in stores:
        copy.wait()


def local(perturbations, control, innovation, precision_field, smooth_kernel, vertical_loc):
    dma = pltpu.SemaphoreType.DMA
    anywhere = pl.BlockSpec(memory_space=pl.ANY)
    increment, gradient = pl.pallas_call(
        kernel,
        out_shape=[
            jax.ShapeDtypeStruct((256, 512), F32),
            jax.ShapeDtypeStruct((512, 512), F32),
        ],
        in_specs=[
            anywhere, anywhere, anywhere, anywhere,
            pl.BlockSpec(memory_space=pltpu.SMEM),
            pl.BlockSpec(memory_space=pltpu.VMEM),
        ],
        out_specs=[anywhere, anywhere],
        scratch_shapes=[
            pltpu.VMEM((4, 512, 128), F32),
            pltpu.VMEM((4, 512, 128), BF16),
            pltpu.VMEM((4, 512, 128), F32),
            pltpu.VMEM((4, 256, 128), F32),
            pltpu.VMEM((4, 256, 128), F32),
            pltpu.VMEM((32, 128, 128), F32),
            pltpu.VMEM((32, 128, 128), F32),
            pltpu.VMEM((32, 144, 256), BF16),
            pltpu.VMEM((2, 3, 512, 512), BF16),
            pltpu.VMEM((2, 3, 256, 256), BF16),
            pltpu.VMEM((2, 3, 256, 256), BF16),
            pltpu.VMEM((16, 128, 128), F32),
            pltpu.VMEM((2, 8, 64, 128), F32),
            pltpu.VMEM((8, 64, 128), F32),
            pltpu.VMEM((8, 64, 128), F32),
            pltpu.VMEM((8, 64, 128), F32),
            pltpu.VMEM((16, 64, 128), F32),
            pltpu.VMEM((16, 64, 128), F32),
            pltpu.VMEM((64, 128), F32),
            pltpu.VMEM((16, 64, 128), F32),
            pltpu.VMEM((16, 64, 128), F32),
            pltpu.VMEM((4, 512, 128), F32),
            pltpu.VMEM((4, 256, 128), F32),
            dma((4, 4)), dma((2, 4)),
            dma((4,)), dma((4,)),
            dma((2,)), dma((2,)),
            dma((1,)), dma((1,)),
            dma((8,)), dma((8,)),
            dma((8,)), dma((8,)),
            dma((8,)), dma((8,)),
            dma((8,)), dma((8,)),
            dma((8,)), dma((8,)),
        ],
        compiler_params=pltpu.CompilerParams(
            collective_id=0, has_side_effects=True, vmem_limit_bytes=48 * 2**20
        ),
        cost_estimate=pl.CostEstimate(flops=20 * 10**9, bytes_accessed=4 * 2**20, transcendentals=0),
        name="increment_and_gradient",
    )(
        control.reshape(512, 512),
        perturbations.reshape(512, 512),
        innovation.reshape(256, 512),
        precision_field.reshape(256, 512),
        smooth_kernel,
        vertical_loc,
    )
    return increment.reshape(16, 16, 512), gradient.reshape(2, 16, 16, 512)


def solution(mesh):
    in_specs = (
        P("mem", None, "tile", None),
        P("mem", None, "tile", None),
        P(None, "tile", None),
        P(None, "tile", None),
        P(),
        P(),
    )
    out_specs = (P(None, "tile", None), P("mem", None, "tile", None))
    return jax.shard_map(local, mesh=mesh, in_specs=in_specs, out_specs=out_specs, check_vma=False)
```

time: 430 us -> 82.1 us (0.19)
  other arithmetic: 154 us -> 0 us
  waiting for transfers between devices: 142 us -> 0 us
  starting transfers between devices: 82.7 us -> 0 us
  Pallas kernels: 0 us -> 73.6 us
  matrix products: 25.8 us -> 0 us
  between operations: 14.5 us -> 0.65 us
    psum x1 -> x0, waiting for transfers between devices: 131 us -> none  [local(): increment = lax.psum(contribution, 'mem')]
    add x6 -> x0, other arithmetic: 128 us -> none  [stencil_step(): total = total + weights[a, b] * padded[:, :, a:a + width, b:b + rows]]
    ppermute x16 -> x0, starting transfers between devices: 82.6 us -> none  [the longest x8 63.5 us: extended_2(): lax.ppermute(head, axis, [((i + 1) % count, i) for i in range(count)])]
    pallas_call x0 -> x1, Pallas kernels: none -> 73.6 us  [local(): pl.pallas_call(kernel, out_shape=[jax.ShapeDtypeStruct((256, 512), F32),...]
    dot_general x2 -> x0, matrix products: 25.8 us -> none  [the longest x1 23 us: local(): jnp.einsum('ml,kmij->klij', vertical_loc, smoothed_back, precision=lax.Pr...]
    reduce_sum x2 -> x0, other arithmetic: 22.8 us -> none  [the longest x1 22.2 us: local(): contribution = jnp.sum(pert_float * localized, axis=0)]
    ppermute x16 -> x0, waiting for transfers between devices: 10.6 us -> none  [the longest x8 9.05 us: extended_2(): lax.ppermute(head, axis, [((i + 1) % count, i) for i in range(count)])]
  transfers between devices with their start and end apart: 17 -> 0, of which waited for: 13 -> 0; matrix products, arithmetic and copies ran while one was open for 1% -> 0% of each run, Pallas kernels for 0% -> 0%
where the time goes in v1:
time: 82.1 us; the launch traced here: 81.8 us
  Pallas kernels  73.6 us (90%)
  local copies, waits for them, and re-layouts  7.49 us (9%)
    pallas_call x1, Pallas kernels, local(): pl.pallas_call(kernel, out_shape=[jax.ShapeDtypeStruct((256, 512), F32),...  73.6 us
    unnamed x14, local copies, waits for them, and re-layouts  7.49 us

profile of v1, /device:TPU:1, one launch (start us, length us, event | category | flops | bytes accessed | tf_op | source)
XLA Modules:
  0.0 81.8 jit_solution(6110877233593565093)
XLA Ops:
  0.6 0.0 copy-start.5
  0.6 0.7 copy-done.5
  1.3 0.0 copy-start
  1.3 1.2 %copy-done = f32[2,16,16,512]{3,2,1,0:T(8,128)S(1)} copy-done((f32[2,16,16,512]{3,2,1,0:T(8,128)S(1)}, f32[2,16,16,512]{3,2,1,0:T(8,128)}, u32[]{:S(2)}) %copy-start) | copy-done | bytes 1048600
  2.5 0.0 copy-start.1
  2.5 1.0 %copy-done.1 = bf16[2,16,16,512]{3,2,1,0:T(8,128)(2,1)S(1)} copy-done((bf16[2,16,16,512]{3,2,1,0:T(8,128)(2,1)S(1)}, bf16[2,16,16,512]{3,2,1,0:T(8,128)(2,1)}, u32[]{:S(2)}) %copy-start.1) | copy-done | bytes 524312
  3.6 0.0 copy-start.2
  3.6 1.0 %copy-done.2 = f32[16,16,512]{2,1,0:T(8,128)S(1)} copy-done((f32[16,16,512]{2,1,0:T(8,128)S(1)}, f32[16,16,512]{2,1,0:T(8,128)}, u32[]{:S(2)}) %copy-start.2) | copy-done | bytes 524312
  4.6 0.0 copy-start.3
  4.6 1.0 %copy-done.3 = f32[16,16,512]{2,1,0:T(8,128)S(1)} copy-done((f32[16,16,512]{2,1,0:T(8,128)S(1)}, f32[16,16,512]{2,1,0:T(8,128)}, u32[]{:S(2)}) %copy-start.3) | copy-done | bytes 524312
  5.7 0.0 copy-start.4
  5.7 0.7 copy-done.4
  6.4 73.6 %increment_and_gradient.1 = (f32[256,512]{1,0:T(8,128)S(1)}, f32[512,512]{1,0:T(8,128)S(1)}) custom-call(f32[512,512]{1,0:T(8,128)S(1)} %bitcast.8, bf16[512,512]{1,0:T(8,128)(2,1)S(1)} %bitcast.9, f32[256,512]{1,0:T(8,128)S(1)} %bitcast.10, f32[256,512]{1,0:T(8,128)S(1)} %bitcast.11, f32[5,5]{1,0:T(8,128)S(1)} %copy-done.5, f32[16,16]{1,0:T(8,128)S(1)} %copy-done.4), custom_call_target="tpu_custom_call" | custom-call | flops 20000000000 | bytes 4194304 | tf_op jit(solution)/shard_map/increment_and_gradient/pallas_call | solution.py:367
  80.0 0.8 copy.10
  80.8 1.0 %copy.11 = f32[2,16,16,512]{3,2,1,0:T(8,128)} copy(f32[2,16,16,512]{3,2,1,0:T(8,128)S(1)} %bitcast.6) | data formatting | bytes 2097152
Async XLA Ops:
  0.6 0.7 copy-start.5
  1.3 1.2 %copy-start = (f32[2,16,16,512]{3,2,1,0:T(8,128)S(1)}, f32[2,16,16,512]{3,2,1,0:T(8,128)}, u32[]{:S(2)}) copy-start(f32[2,16,16,512]{3,2,1,0:T(8,128)} %param.7) | copy-start | bytes 3145732
  2.5 1.0 %copy-start.1 = (bf16[2,16,16,512]{3,2,1,0:T(8,128)(2,1)S(1)}, bf16[2,16,16,512]{3,2,1,0:T(8,128)(2,1)}, u32[]{:S(2)}) copy-start(bf16[2,16,16,512]{3,2,1,0:T(8,128)(2,1)} %param.6) | copy-start | bytes 1572868
  3.6 1.0 %copy-start.2 = (f32[16,16,512]{2,1,0:T(8,128)S(1)}, f32[16,16,512]{2,1,0:T(8,128)}, u32[]{:S(2)}) copy-start(f32[16,16,512]{2,1,0:T(8,128)} %param.8) | copy-start | bytes 1572868
  4.6 1.0 %copy-start.3 = (f32[16,16,512]{2,1,0:T(8,128)S(1)}, f32[16,16,512]{2,1,0:T(8,128)}, u32[]{:S(2)}) copy-start(f32[16,16,512]{2,1,0:T(8,128)} %param.9) | copy-start | bytes 1572868
  5.7 0.7 copy-start.4

commit v2 on v1

v2 whole, which is shorter than its diff:
```python
import functools

import jax
import jax.numpy as jnp
from jax import lax
from jax.experimental import pallas as pl
from jax.experimental.pallas import tpu as pltpu
from jax.sharding import PartitionSpec as P

MESH = pl.DeviceIdType.MESH
HIGHEST = lax.Precision.HIGHEST
F32 = jnp.float32
BF16 = jnp.bfloat16


def lanes_of(shape):
    return lax.broadcasted_iota(jnp.int32, shape, len(shape) - 1)


def rows_of(shape):
    return lax.broadcasted_iota(jnp.int32, shape, len(shape) - 2)


def roll(x, shift):
    return pltpu.roll(x, shift % x.shape[-1], x.ndim - 1)


def composed_rows(sk, flip, variant):
    shape = (16, 1024)
    lane = lanes_of(shape)
    col = lane % 32
    start = jnp.where(lane == 264 + rows_of(shape), 1.0, 0.0).astype(F32)
    if variant == 0:
        inside = col >= 8
    elif variant == 2:
        inside = col < 24
    else:
        inside = None

    def tap(a, b):
        return sk[4 - a, 4 - b] if flip else sk[a, b]

    def one_pass(step, r):
        moved = [roll(r, 32 * (a - 2)) if a != 2 else r for a in range(5)]
        out = None
        for b in range(5):
            part = moved[0] * tap(0, b)
            for a in range(1, 5):
                part = part + moved[a] * tap(a, b)
            part = roll(part, b - 2) if b != 2 else part
            out = part if out is None else out + part
        if inside is not None:
            out = jnp.where(inside, out, 0.0)
        return out

    r = lax.fori_loop(0, 4, one_pass, start)
    total = sk[0, 0]
    for n in range(1, 25):
        total = total + sk[n // 5, n % 5]
    total = jnp.full((16, 1024), total, F32)
    square = total * total
    return r / (square * square)


def split(x):
    hi = x.astype(BF16)
    lo = (x - hi.astype(F32)).astype(BF16)
    return hi, lo


def kernel(
    ctl_h, pert_h, innov_h, prec_h, sk, vloc,
    inc_h, grad_h,
    ctl_v, pert_v, pert_f, innov_v, prec_v, pt, xb, weights, back, field,
    contrib, core_in, chip_sum, parts_in, contrib_h, core_in_h, chip_sum_h, parts_h,
    inc_all, halo_w, own_w, prec_p, innov_p, grad_v, inc_v,
    in_sem, out_sem, p_send, p_recv, k_send, k_recv, r_send, r_recv, s_send, s_recv,
    a_send, a_recv, h_send, h_recv, f_send, f_recv, g_send, g_recv,
):
    m = lax.axis_index("mem")
    t = lax.axis_index("tile")
    tiles = lax.axis_size("tile")
    right = lax.rem(t + 1, tiles)
    left = lax.rem(t + tiles - 1, tiles)
    chip = m // 2
    core = m % 2
    sibling = 2 * chip + 1 - core
    upper = chip // 4
    beside = jnp.where(chip < 4, left, right)
    opposite = jnp.where(chip < 4, right, left)

    loads = [
        [
            pltpu.make_async_copy(src.at[:, pl.ds(128 * q, 128)], dst.at[q], in_sem.at[n, q])
            for q in range(4)
        ]
        for n, (src, dst) in enumerate(
            [(pert_h, pert_v), (ctl_h, ctl_v), (innov_h, innov_v), (prec_h, prec_v)]
        )
    ]
    for load in loads:
        for copy in load:
            copy.start()

    def arrive(n):
        for copy in loads[n]:
            copy.wait()

    def peer(d):
        other = jnp.bitwise_xor(chip, d)
        return other, 2 * other + core

    barrier = pltpu.get_barrier_semaphore()

    def greet(mem, tile):
        pl.semaphore_signal(barrier, inc=1, device_id=(mem, tile), device_id_type=MESH)

    greet(sibling, t)
    for d in range(1, 8):
        greet(peer(d)[1], t)
    for k in range(8):
        greet(2 * k + core, beside)
    for k in range(4):
        greet(2 * (4 * upper + k) + core, opposite)

    pick = jnp.where(rows_of((128, 16)) % 16 == lanes_of((128, 16)), 1.0, 0.0).astype(F32)
    wide = jnp.dot(pick, vloc[...], precision=HIGHEST, preferred_element_type=F32)
    spread = jnp.where(lanes_of((16, 128)) % 16 == rows_of((16, 128)), 1.0, 0.0).astype(F32)
    full = jnp.dot(wide, spread, precision=HIGHEST, preferred_element_type=F32)
    same = rows_of((128, 128)) // 16 == lanes_of((128, 128)) // 16
    mix = jnp.where(same, full, 0.0)

    def columns(ref, i, count):
        return [ref[q, pl.ds(i, count, stride=16), :] for q in range(4)]

    def remote(src, dst, send, recv, mem, tile):
        return pltpu.make_async_remote_copy(
            src_ref=src, dst_ref=dst, send_sem=send, recv_sem=recv,
            device_id=(mem, tile), device_id_type=MESH,
        )

    def outward(ref, first, send, recv):
        to_right = first >= 16
        target = first - 16 if to_right else first + 16
        return remote(
            ref.at[pl.ds(first, 4)], ref.at[pl.ds(target, 4)], send, recv, m,
            right if to_right else left,
        )

    arrive(0)
    p_copies = []
    for n, first in enumerate((16, 12, 20, 8)):
        if n == 0:
            pert_f[...] = pert_v[...].astype(F32)
        for i in range(first, first + 4):
            pt[i] = jnp.concatenate(columns(pert_f, i - 8, 32), axis=0).T
        if n == 0:
            pl.semaphore_wait(barrier, 20)
        copy = outward(pt, first, p_send.at[n], p_recv.at[n])
        copy.start()
        p_copies.append(copy)

    lane8 = lanes_of((8, 128))

    def prepare(index, x):
        top = jnp.where(lane8 >= 32, roll(x[120:128], 32), 0.0)
        bottom = jnp.where(lane8 < 96, roll(x[0:8], -32), 0.0)
        hi, lo = split(jnp.concatenate([top, x, bottom], axis=0))
        xb[index, :, 0:128] = hi
        xb[index, :, 128:256] = lo

    def each(first, last, body):
        def step(i, carry):
            for n in range(4):
                body(4 * i + n)
            return carry

        lax.fori_loop(first // 4, last // 4, step, 0)

    arrive(1)
    for i in range(16):
        x = jnp.concatenate(columns(ctl_v, i, 32), axis=0)
        x = jnp.dot(mix, x, precision=HIGHEST, preferred_element_type=F32)
        prepare(8 + i, x.T)

    def build(direction, variant):
        base = composed_rows(sk, direction == 1, variant)
        for i in range(16):
            hi, lo = split(roll(base, 32 * i) if i else base)
            weights[direction, variant, 16 * i : 16 * i + 16, :] = hi
            weights[direction, variant, 256 + 16 * i : 272 + 16 * i, :] = lo

    for variant in range(3):
        build(0, variant)

    lane3 = lanes_of((1, 1, 128))

    def smooth(direction, spans, lons, put):
        def at(variant, b):
            w = weights.at[direction, variant]
            parts = [
                jnp.concatenate(
                    [w[at : at + 16 * (z - a), 32 * lo : 32 * hi] for lo, hi, _ in spans], axis=1
                )
                for part in range(2)
                for a, z in lons
                for at in [256 * part + 16 * a]
            ]
            lhs = jnp.concatenate(parts, axis=0)
            rhs = jnp.concatenate(
                [
                    xb[x : x + hi - lo, 16 * b : 16 * b + 32, :].reshape(32 * (hi - lo), 256)
                    for lo, hi, x in spans
                ],
                axis=0,
            )
            out = jnp.dot(lhs, rhs, preferred_element_type=F32)
            half = out.shape[0] // 2
            out = out[:half, :128] + out[:half, 128:] + out[half:, :128]
            return out.reshape(half // 16, 16, 128)

        for b in range(8):
            value = at(1, b)
            if b == 0:
                value = jnp.where(lane3 < 32, at(0, b), value)
            if b == 7:
                value = jnp.where(lane3 >= 96, at(2, b), value)
            done = 0
            for a, z in lons:
                put(a, z, 16 * b, value[done : done + z - a])
                done += z - a

    def put(a, z, row, value):
        field[8 + a : 8 + z, row : row + 16, :] = value

    def put_left(a, z, row, value):
        field[a - 8 : z - 8, row : row + 16, :] = value

    def put_right(a, z, row, value):
        field[24 + a : 24 + z, row : row + 16, :] = value

    def add(a, z, row, value):
        field[8 + a : 8 + z, row : row + 16, :] = field[8 + a : 8 + z, row : row + 16, :] + value

    every = [(0, 16)]
    outer = [(0, 4), (12, 16)]
    smooth(0, [(8, 24, 8)], every, put)
    smooth(0, [(24, 32, 8)], [(8, 16)], put_left)
    smooth(0, [(0, 8, 16)], [(0, 8)], put_right)

    first_half = lanes_of((64, 128)) % 32 < 16
    inner_first = [[4 + k for k in range(8)], [k if k < 4 else k + 8 for k in range(8)]]

    halo_first = [
        [28 + k if k < 4 else k - 4 for k in range(8)],
        [24 + k if k < 4 else k for k in range(8)],
    ]

    def members(i):
        x = pt[i] * field[i]
        top, bottom = x[0:64], x[64:128]
        here = jnp.where(first_half, top, bottom)
        there = jnp.where(first_half, roll(top, -16), roll(bottom, 16))
        return here + there

    def to_sibling(src, dst, n):
        copy = remote(src.at[1 - core], dst, k_send.at[n], k_recv.at[n], sibling, t)
        copy.start()
        return copy

    def contribute_halo(g):
        for k, i in enumerate(halo_first[g]):
            both = members(i)
            contrib_h[g, 0, k] = both[0:32]
            contrib_h[g, 1, k] = both[32:64]
        return to_sibling(contrib_h.at[g], core_in_h.at[g], g)

    def scatter_halo(g, copy):
        copy.wait()
        chip_sum_h[g] = contrib_h[g, core] + core_in_h[g]
        copies = []
        for k in range(8):
            copy = remote(
                chip_sum_h.at[g, k], parts_h.at[g, chip], s_send.at[g, k], s_recv.at[g, chip],
                2 * k + core, right if k < 4 else left,
            )
            copy.start()
            copies.append(copy)
        return copies

    def spread_total(g, copies):
        for copy in copies:
            copy.wait_send()
        total = chip_sum[chip, g]
        for d in range(1, 8):
            total = total + parts_in[peer(d)[0], g]
        for k in range(8):
            remote(
                chip_sum_h.at[g, k], parts_h.at[g, k], s_send.at[g, k], s_recv.at[g, k], m, beside
            ).wait_recv()
        for k in range(8):
            total = total + parts_h[g, k]
        inc_all[g, chip, core] = total
        lon = 4 + chip if g == 0 else chip + 8 * (chip // 4)
        own_w[g] = prec_p[lon, core] * (total - innov_p[lon, core])
        a_copies = []
        for d in range(1, 8):
            mem = peer(d)[1]
            piece = inc_all.at[g, chip, core]
            copy = remote(piece, piece, a_send.at[g, d], a_recv.at[g, d], mem, t)
            copy.start()
            a_copies.append(copy)
        h_copies = []
        for d in range(8):
            copy = remote(
                own_w.at[g], halo_w.at[g, chip, core],
                h_send.at[g, d], h_recv.at[g, chip], peer(d)[1], beside,
            )
            copy.start()
            h_copies.append(copy)
        return a_copies, h_copies

    def pass_total(g, a_copies):
        for copy in a_copies:
            copy.wait()
        piece = inc_all.at[g, pl.ds(0, 8), core]
        copy = remote(piece, piece, f_send.at[g], f_recv.at[g], sibling, t)
        copy.start()
        return copy

    def pass_halo(g, h_copies):
        for copy in h_copies:
            copy.wait_send()
        for k in range(8):
            remote(
                own_w.at[g], halo_w.at[g, chip, core],
                h_send.at[g, k], h_recv.at[g, k], m, beside,
            ).wait_recv()
        piece = halo_w.at[g, pl.ds(0, 8), core]
        copy = remote(piece, piece, g_send.at[g], g_recv.at[g], sibling, t)
        copy.start()
        return copy

    for g in range(2):
        for k, i in enumerate(inner_first[g]):
            both = members(8 + i)
            contrib[0, k, g] = both[0:32]
            contrib[1, k, g] = both[32:64]
    k_copy = to_sibling(contrib, core_in, 2)

    def pack(ref, out, i):
        parts = [p for p in columns(ref, i, 16) for _ in range(2)]
        x = jnp.concatenate(parts, axis=0).T
        x = jnp.where(first_half, x[0:64], x[64:128])
        out[i, 0] = x[0:32]
        out[i, 1] = x[32:64]

    arrive(2)
    arrive(3)
    for i in range(8):
        pack(innov_v, innov_p, i)
        pack(prec_v, prec_p, i)

    k_copy.wait()
    chip_sum[...] = contrib[core] + core_in[...]
    r_copies = []
    for d in range(1, 8):
        other, mem = peer(d)
        copy = remote(
            chip_sum.at[other], parts_in.at[chip], r_send.at[d], r_recv.at[d], mem, t
        )
        copy.start()
        r_copies.append(copy)

    for copy in p_copies[:2]:
        copy.wait()
    k_copy_0 = contribute_halo(0)
    for i in range(8, 16):
        pack(innov_v, innov_p, i)
        pack(prec_v, prec_p, i)
    s_copies_0 = scatter_halo(0, k_copy_0)
    for copy in p_copies[2:]:
        copy.wait()
    k_copy_1 = contribute_halo(1)
    s_copies_1 = scatter_halo(1, k_copy_1)

    build(1, 1)
    for copy in r_copies:
        copy.wait()
    a_copies_0, h_copies_0 = spread_total(0, s_copies_0)
    build(1, 0)
    build(1, 2)
    a_copies_1, h_copies_1 = spread_total(1, s_copies_1)
    f_copy_0 = pass_total(0, a_copies_0)
    g_copy_0 = pass_halo(0, h_copies_0)

    def unpack(w):
        top = jnp.where(first_half, w, roll(w, 16))
        bottom = jnp.where(first_half, roll(w, -16), w)
        return jnp.concatenate([top, bottom], axis=0)

    def own_input(g, k, lon):
        total = inc_all[g, k].reshape(64, 128)
        w = prec_p[lon].reshape(64, 128) * (total - innov_p[lon].reshape(64, 128))
        prepare(8 + lon, pt[8 + lon] * unpack(w))

    def halo_input(g, k, index):
        prepare(index, pt[index] * unpack(halo_w[g, k].reshape(64, 128)))

    def show(g):
        for k, i in enumerate(inner_first[g]):
            x = unpack(inc_all[g, k].reshape(64, 128)).T
            for q in range(4):
                inc_v[q, pl.ds(i, 16, stride=16), :] = x[32 * q : 32 * q + 16]

    f_copy_0.wait()
    each(0, 8, lambda k: own_input(0, k, k + 4))
    smooth(1, [(12, 20, 12)], every, put)
    g_copy_0.wait()
    each(0, 4, lambda k: halo_input(0, k, 28 + k))
    each(4, 8, lambda k: halo_input(0, k, k - 4))
    smooth(1, [(0, 4, 0), (28, 32, 28)], outer, add)
    show(0)

    f_copy_1 = pass_total(1, a_copies_1)
    g_copy_1 = pass_halo(1, h_copies_1)
    f_copy_1.wait()
    each(0, 4, lambda k: own_input(1, k, k))
    each(4, 8, lambda k: own_input(1, k, k + 8))
    g_copy_1.wait()
    each(0, 4, lambda k: halo_input(1, k, 24 + k))
    each(4, 8, lambda k: halo_input(1, k, k))
    smooth(1, [(4, 12, 4), (20, 28, 20)], every, add)

    show(1)
    stores = []

    def store(src, dst, n):
        for q in range(4):
            copy = pltpu.make_async_copy(src.at[q], dst.at[:, pl.ds(128 * q, 128)], out_sem.at[n, q])
            copy.start()
            stores.append(copy)

    store(inc_v, inc_h, 0)

    hi, lo = split(mix.T)
    back[0:128, 0:128] = hi
    back[0:128, 128:256] = hi
    back[128:256, 0:128] = lo
    back[128:256, 128:256] = jnp.zeros((128, 128), BF16)
    for i in range(0, 16, 2):
        hi, lo = split(field[8 + i : 10 + i].reshape(256, 128))
        x = lax.dot_general(
            back[...], jnp.concatenate([hi, lo], axis=1), (((1,), (1,)), ((), ())),
            preferred_element_type=F32,
        )
        x = x[0:128] + x[128:256]
        for n in range(2):
            old = columns(ctl_v, i + n, 32)
            for q in range(4):
                grad_v[q, pl.ds(i + n, 32, stride=16), :] = (
                    x[32 * q : 32 * q + 32, 128 * n : 128 * n + 128] + old[q]
                )
    store(grad_v, grad_h, 1)
    for copy in stores:
        copy.wait()


def local(perturbations, control, innovation, precision_field, smooth_kernel, vertical_loc):
    dma = pltpu.SemaphoreType.DMA
    anywhere = pl.BlockSpec(memory_space=pltpu.HBM)
    increment, gradient = pl.pallas_call(
        kernel,
        out_shape=[
            jax.ShapeDtypeStruct((256, 512), F32),
            jax.ShapeDtypeStruct((512, 512), F32),
        ],
        in_specs=[
            anywhere, anywhere, anywhere, anywhere,
            pl.BlockSpec(memory_space=pltpu.SMEM),
            pl.BlockSpec(memory_space=pltpu.VMEM),
        ],
        out_specs=[anywhere, anywhere],
        scratch_shapes=[
            pltpu.VMEM((4, 512, 128), F32),
            pltpu.VMEM((4, 512, 128), BF16),
            pltpu.VMEM((4, 512, 128), F32),
            pltpu.VMEM((4, 256, 128), F32),
            pltpu.VMEM((4, 256, 128), F32),
            pltpu.VMEM((32, 128, 128), F32),
            pltpu.VMEM((32, 144, 256), BF16),
            pltpu.VMEM((2, 3, 512, 1024), BF16),
            pltpu.VMEM((256, 256), BF16),
            pltpu.VMEM((32, 128, 128), F32),
            pltpu.VMEM((2, 8, 2, 32, 128), F32),
            pltpu.VMEM((8, 2, 32, 128), F32),
            pltpu.VMEM((8, 2, 32, 128), F32),
            pltpu.VMEM((8, 2, 32, 128), F32),
            pltpu.VMEM((2, 2, 8, 32, 128), F32),
            pltpu.VMEM((2, 8, 32, 128), F32),
            pltpu.VMEM((2, 8, 32, 128), F32),
            pltpu.VMEM((2, 8, 32, 128), F32),
            pltpu.VMEM((2, 8, 2, 32, 128), F32),
            pltpu.VMEM((2, 8, 2, 32, 128), F32),
            pltpu.VMEM((2, 32, 128), F32),
            pltpu.VMEM((16, 2, 32, 128), F32),
            pltpu.VMEM((16, 2, 32, 128), F32),
            pltpu.VMEM((4, 512, 128), F32),
            pltpu.VMEM((4, 256, 128), F32),
            dma((4, 4)), dma((2, 4)),
            dma((4,)), dma((4,)),
            dma((3,)), dma((3,)),
            dma((8,)), dma((8,)),
            dma((2, 8)), dma((2, 8)),
            dma((2, 8)), dma((2, 8)),
            dma((2, 8)), dma((2, 8)),
            dma((2,)), dma((2,)),
            dma((2,)), dma((2,)),
        ],
        compiler_params=pltpu.CompilerParams(
            collective_id=0, has_side_effects=True, vmem_limit_bytes=64 * 2**20
        ),
        cost_estimate=pl.CostEstimate(flops=20 * 10**9, bytes_accessed=4 * 2**20, transcendentals=0),
        name="increment_and_gradient",
    )(
        control.reshape(512, 512),
        perturbations.reshape(512, 512),
        innovation.reshape(256, 512),
        precision_field.reshape(256, 512),
        smooth_kernel,
        vertical_loc,
    )
    return increment.reshape(16, 16, 512), gradient.reshape(2, 16, 16, 512)


def solution(mesh):
    in_specs = (
        P("mem", None, "tile", None),
        P("mem", None, "tile", None),
        P(None, "tile", None),
        P(None, "tile", None),
        P(),
        P(),
    )
    out_specs = (P(None, "tile", None), P("mem", None, "tile", None))
    return jax.shard_map(local, mesh=mesh, in_specs=in_specs, out_specs=out_specs, check_vma=False)
```

time: 82.1 us -> 59.4 us (0.72)
  Pallas kernels: 73.6 us -> 55.5 us
  local copies, waits for them, and re-layouts: 7.49 us -> 2.94 us
    pallas_call x1, Pallas kernels: 73.6 us -> 55.5 us  [local(): pl.pallas_call(kernel, out_shape=[jax.ShapeDtypeStruct((256, 512), F32),...]
    unnamed x14 -> x4, local copies, waits for them, and re-layouts: 7.49 us -> 2.94 us
where the time goes in v2:
time: 59.4 us; the launch traced here: 59.1 us
  Pallas kernels  55.5 us (93%)
  local copies, waits for them, and re-layouts  2.94 us (5%)
  between operations  0.65 us (1%)
    pallas_call x1, Pallas kernels, local(): pl.pallas_call(kernel, out_shape=[jax.ShapeDtypeStruct((256, 512), F32),...  55.5 us
    unnamed x4, local copies, waits for them, and re-layouts  2.94 us

profile of v2, /device:TPU:1, one launch (start us, length us, event | category | flops | bytes accessed | tf_op | source)
XLA Modules:
  0.0 59.1 jit_solution(13492123174991909185)
XLA Ops:
  0.6 55.5 %increment_and_gradient.1 = (f32[256,512]{1,0:T(8,128)}, f32[512,512]{1,0:T(8,128)}) custom-call(f32[512,512]{1,0:T(8,128)} %bitcast.8, bf16[512,512]{1,0:T(8,128)(2,1)} %bitcast.9, f32[256,512]{1,0:T(8,128)} %bitcast.10, f32[256,512]{1,0:T(8,128)} %bitcast.11, f32[5,5]{1,0:T(8,128)} %sk.1, f32[16,16]{1,0:T(8,128)} %vloc.1), custom_call_target="tpu_custom_call" | custom-call | flops 20000000000 | bytes 4194304 | tf_op jit(solution)/shard_map/increment_and_gradient/pallas_call | solution.py:472
  56.1 0.0 copy-start
  56.1 2.0 %copy.10 = f32[16,16,512]{2,1,0:T(8,128)} copy(f32[16,16,512]{2,1,0:T(8,128)} %bitcast.7) | data formatting | bytes 1048576
  58.1 0.0 copy-done
  58.1 1.0 %copy.11 = f32[2,16,16,512]{3,2,1,0:T(8,128)} copy(f32[2,16,16,512]{3,2,1,0:T(8,128)S(1)} %bitcast.6) | data formatting | bytes 2097152
Async XLA Ops:
  56.1 2.0 %copy-start = (f32[512,512]{1,0:T(8,128)S(1)}, f32[512,512]{1,0:T(8,128)}, u32[]{:S(2)}) copy-start(f32[512,512]{1,0:T(8,128)} %get-tuple-element.5) | copy-start | bytes 3145732

commit v3 on v2

--- a/solution.py
+++ b/solution.py
@@ -25,17 +25,14 @@
     return pltpu.roll(x, shift % x.shape[-1], x.ndim - 1)
 
 
-def composed_rows(sk, flip, variant):
-    shape = (16, 1024)
+def composed_rows(sk, flip):
+    shape = (24, 640)
     lane = lanes_of(shape)
+    band = rows_of(shape) // 8
+    j = rows_of(shape) % 8 + jnp.where(band == 2, 8, 0)
     col = lane % 32
-    start = jnp.where(lane == 264 + rows_of(shape), 1.0, 0.0).astype(F32)
-    if variant == 0:
-        inside = col >= 8
-    elif variant == 2:
-        inside = col < 24
-    else:
-        inside = None
+    start = jnp.where(lane == 264 + j, 1.0, 0.0).astype(F32)
+    outside = ((band == 0) & (col < 8)) | ((band == 2) & (col >= 24))
 
     def tap(a, b):
         return sk[4 - a, 4 - b] if flip else sk[a, b]
@@ -49,15 +46,13 @@
                 part = part + moved[a] * tap(a, b)
             part = roll(part, b - 2) if b != 2 else part
             out = part if out is None else out + part
-        if inside is not None:
-            out = jnp.where(inside, out, 0.0)
-        return out
+        return jnp.where(outside, 0.0, out)
 
     r = lax.fori_loop(0, 4, one_pass, start)
     total = sk[0, 0]
     for n in range(1, 25):
         total = total + sk[n // 5, n % 5]
-    total = jnp.full((16, 1024), total, F32)
+    total = jnp.full(shape, total, F32)
     square = total * total
     return r / (square * square)
 
@@ -70,11 +65,11 @@
 
 def kernel(
     ctl_h, pert_h, innov_h, prec_h, sk, vloc,
-    inc_h, grad_h,
+    inc_v, grad_v,
     ctl_v, pert_v, pert_f, innov_v, prec_v, pt, xb, weights, back, field,
     contrib, core_in, chip_sum, parts_in, contrib_h, core_in_h, chip_sum_h, parts_h,
-    inc_all, halo_w, own_w, prec_p, innov_p, grad_v, inc_v,
-    in_sem, out_sem, p_send, p_recv, k_send, k_recv, r_send, r_recv, s_send, s_recv,
+    inc_all, halo_w, own_w, prec_p, innov_p,
+    in_sem, p_send, p_recv, k_send, k_recv, r_send, r_recv, s_send, s_recv,
     a_send, a_recv, h_send, h_recv, f_send, f_recv, g_send, g_recv,
 ):
     m = lax.axis_index("mem")
@@ -183,15 +178,27 @@
         x = jnp.dot(mix, x, precision=HIGHEST, preferred_element_type=F32)
         prepare(8 + i, x.T)
 
-    def build(direction, variant):
-        base = composed_rows(sk, direction == 1, variant)
-        for i in range(16):
-            hi, lo = split(roll(base, 32 * i) if i else base)
-            weights[direction, variant, 16 * i : 16 * i + 16, :] = hi
-            weights[direction, variant, 256 + 16 * i : 272 + 16 * i, :] = lo
-
-    for variant in range(3):
-        build(0, variant)
+    def build(direction):
+        rows = composed_rows(sk, direction == 1)
+        first, inside, last = rows[0:8], rows[8:16], rows[16:24]
+        shifted = roll(inside, 8)
+        for variant, halves in enumerate([(first, shifted), (inside, shifted), (inside, last)]):
+            base = jnp.concatenate(halves, axis=0)
+            for n in range(4):
+                for part, value in enumerate(split(roll(base, 32 * n) if n else base)):
+                    for i in range(n, 16, 4):
+                        at = 256 * part + 16 * i
+                        lane = 32 * (i - n)
+                        if lane:
+                            weights[direction, variant, at : at + 16, 0:lane] = jnp.zeros((16, lane), BF16)
+                        weights[direction, variant, at : at + 16, lane : lane + 640] = value
+                        rest = 1024 - lane - 640
+                        if rest:
+                            weights[direction, variant, at : at + 16, lane + 640 : 1024] = jnp.zeros(
+                                (16, rest), BF16
+                            )
+
+    build(0)
 
     lane3 = lanes_of((1, 1, 128))
 
@@ -303,13 +310,6 @@
         inc_all[g, chip, core] = total
         lon = 4 + chip if g == 0 else chip + 8 * (chip // 4)
         own_w[g] = prec_p[lon, core] * (total - innov_p[lon, core])
-        a_copies = []
-        for d in range(1, 8):
-            mem = peer(d)[1]
-            piece = inc_all.at[g, chip, core]
-            copy = remote(piece, piece, a_send.at[g, d], a_recv.at[g, d], mem, t)
-            copy.start()
-            a_copies.append(copy)
         h_copies = []
         for d in range(8):
             copy = remote(
@@ -318,6 +318,13 @@
             )
             copy.start()
             h_copies.append(copy)
+        a_copies = []
+        for d in range(1, 8):
+            mem = peer(d)[1]
+            piece = inc_all.at[g, chip, core]
+            copy = remote(piece, piece, a_send.at[g, d], a_recv.at[g, d], mem, t)
+            copy.start()
+            a_copies.append(copy)
         return a_copies, h_copies
 
     def pass_total(g, a_copies):
@@ -357,7 +364,7 @@
 
     arrive(2)
     arrive(3)
-    for i in range(8):
+    for i in range(4):
         pack(innov_v, innov_p, i)
         pack(prec_v, prec_p, i)
 
@@ -375,21 +382,28 @@
     for copy in p_copies[:2]:
         copy.wait()
     k_copy_0 = contribute_halo(0)
-    for i in range(8, 16):
+    for i in range(4, 10):
         pack(innov_v, innov_p, i)
         pack(prec_v, prec_p, i)
     s_copies_0 = scatter_halo(0, k_copy_0)
+    for i in range(10, 16):
+        pack(innov_v, innov_p, i)
+        pack(prec_v, prec_p, i)
     for copy in p_copies[2:]:
         copy.wait()
     k_copy_1 = contribute_halo(1)
+    build(1)
     s_copies_1 = scatter_halo(1, k_copy_1)
 
-    build(1, 1)
+    hi, lo = split(mix.T)
+    back[0:128, 0:128] = hi
+    back[0:128, 128:256] = hi
+    back[128:256, 0:128] = lo
+    back[128:256, 128:256] = jnp.zeros((128, 128), BF16)
+
     for copy in r_copies:
         copy.wait()
     a_copies_0, h_copies_0 = spread_total(0, s_copies_0)
-    build(1, 0)
-    build(1, 2)
     a_copies_1, h_copies_1 = spread_total(1, s_copies_1)
     f_copy_0 = pass_total(0, a_copies_0)
     g_copy_0 = pass_halo(0, h_copies_0)
@@ -427,27 +441,13 @@
     f_copy_1.wait()
     each(0, 4, lambda k: own_input(1, k, k))
     each(4, 8, lambda k: own_input(1, k, k + 8))
+    smooth(1, [(8, 12, 8), (20, 24, 20)], every, add)
     g_copy_1.wait()
     each(0, 4, lambda k: halo_input(1, k, 24 + k))
     each(4, 8, lambda k: halo_input(1, k, k))
-    smooth(1, [(4, 12, 4), (20, 28, 20)], every, add)
+    smooth(1, [(4, 8, 4), (24, 28, 24)], every, add)
 
     show(1)
-    stores = []
-
-    def store(src, dst, n):
-        for q in range(4):
-            copy = pltpu.make_async_copy(src.at[q], dst.at[:, pl.ds(128 * q, 128)], out_sem.at[n, q])
-            copy.start()
-            stores.append(copy)
-
-    store(inc_v, inc_h, 0)
-
-    hi, lo = split(mix.T)
-    back[0:128, 0:128] = hi
-    back[0:128, 128:256] = hi
-    back[128:256, 0:128] = lo
-    back[128:256, 128:256] = jnp.zeros((128, 128), BF16)
     for i in range(0, 16, 2):
         hi, lo = split(field[8 + i : 10 + i].reshape(256, 128))
         x = lax.dot_general(
@@ -461,9 +461,6 @@
                 grad_v[q, pl.ds(i + n, 32, stride=16), :] = (
                     x[32 * q : 32 * q + 32, 128 * n : 128 * n + 128] + old[q]
                 )
-    store(grad_v, grad_h, 1)
-    for copy in stores:
-        copy.wait()
 
 
 def local(perturbations, control, innovation, precision_field, smooth_kernel, vertical_loc):
@@ -472,15 +469,15 @@
     increment, gradient = pl.pallas_call(
         kernel,
         out_shape=[
-            jax.ShapeDtypeStruct((256, 512), F32),
-            jax.ShapeDtypeStruct((512, 512), F32),
+            pltpu.VMEM((4, 256, 128), F32),
+            pltpu.VMEM((4, 512, 128), F32),
         ],
         in_specs=[
             anywhere, anywhere, anywhere, anywhere,
             pl.BlockSpec(memory_space=pltpu.SMEM),
             pl.BlockSpec(memory_space=pltpu.VMEM),
         ],
-        out_specs=[anywhere, anywhere],
+        out_specs=[pl.BlockSpec(memory_space=pltpu.VMEM)] * 2,
         scratch_shapes=[
             pltpu.VMEM((4, 512, 128), F32),
             pltpu.VMEM((4, 512, 128), BF16),
@@ -505,9 +502,7 @@
             pltpu.VMEM((2, 32, 128), F32),
             pltpu.VMEM((16, 2, 32, 128), F32),
             pltpu.VMEM((16, 2, 32, 128), F32),
-            pltpu.VMEM((4, 512, 128), F32),
-            pltpu.VMEM((4, 256, 128), F32),
-            dma((4, 4)), dma((2, 4)),
+            dma((4, 4)),
             dma((4,)), dma((4,)),
             dma((3,)), dma((3,)),
             dma((8,)), dma((8,)),
@@ -518,7 +513,7 @@
             dma((2,)), dma((2,)),
         ],
         compiler_params=pltpu.CompilerParams(
-            collective_id=0, has_side_effects=True, vmem_limit_bytes=64 * 2**20
+            collective_id=0, has_side_effects=True, vmem_limit_bytes=58 * 2**20
         ),
         cost_estimate=pl.CostEstimate(flops=20 * 10**9, bytes_accessed=4 * 2**20, transcendentals=0),
         name="increment_and_gradient",
@@ -530,6 +525,8 @@
         smooth_kernel,
         vertical_loc,
     )
+    increment = jnp.concatenate([increment[q] for q in range(4)], axis=1)
+    gradient = jnp.concatenate([gradient[q] for q in range(4)], axis=1)
     return increment.reshape(16, 16, 512), gradient.reshape(2, 16, 16, 512)
 
 

time: 59.4 us -> 57.4 us (0.966)
  local copies, waits for them, and re-layouts: 2.94 us -> 0.11 us
  other arithmetic: 0 us -> 1.87 us
  Pallas kernels: 55.5 us -> 54 us
    unnamed x4 -> x0, local copies, waits for them, and re-layouts: 2.94 us -> none
    concatenate x0 -> x2, other arithmetic: none -> 1.87 us  [the longest x1 1.04 us: local(): gradient = jnp.concatenate([gradient[q] for q in range(4)], axis=1)]
    pallas_call x1, Pallas kernels: 55.5 us -> 54 us  [local(): pl.pallas_call(kernel, out_shape=[pltpu.VMEM((4, 256, 128), F32), pltpu.V...]
where the time goes in v3:
time: 57.4 us; the launch traced here: 56.6 us
  Pallas kernels  54 us (94%)
  other arithmetic  1.87 us (3%)
  between operations  0.65 us (1%)
    pallas_call x1, Pallas kernels, local(): pl.pallas_call(kernel, out_shape=[pltpu.VMEM((4, 256, 128), F32), pltpu.V...  54 us

profile of v3, /device:TPU:1, one launch (start us, length us, event | category | flops | bytes accessed | tf_op | source)
XLA Modules:
  0.0 56.6 jit_solution(12086620509369881926)
XLA Ops:
  0.6 54.0 %increment_and_gradient.1 = (f32[4,256,128]{2,1,0:T(8,128)S(1)}, f32[4,512,128]{2,1,0:T(8,128)S(1)}) custom-call(f32[512,512]{1,0:T(8,128)} %bitcast.20, bf16[512,512]{1,0:T(8,128)(2,1)} %bitcast.21, f32[256,512]{1,0:T(8,128)} %bitcast.22, f32[256,512]{1,0:T(8,128)} %bitcast.23, f32[5,5]{1,0:T(8,128)} %sk.1, f32[16,16]{1,0:T(8,128)} %vloc.1), custom_call_target="tpu_custom_call" | custom-call | flops 20000000000 | bytes 4194304 | tf_op jit(solution)/shard_map/increment_and_gradient/pallas_call | solution.py:469
  54.7 0.8 %pad_maximum_fusion.1 = f32[16,16,512]{2,1,0:T(8,128)} fusion(f32[16,16,128]{2,1,0:T(8,128)S(1)} %bitcast.17, f32[16,16,128]{2,1,0:T(8,128)S(1)} %bitcast.18, f32[16,16,128]{2,1,0:T(8,128)S(1)} %bitcast.19, f32[16,16,128]{2,1,0:T(8,128)S(1)} %bitcast.16), kind=kLoop, calls=%fused_computation.1 | loop fusion | flops 393216 | bytes 1048576 | tf_op jit(solution)/shard_map/concatenate | solution.py:528
  55.5 0.1 fusion
  55.6 1.0 %pad_maximum_fusion = f32[2,16,16,512]{3,2,1,0:T(8,128)} fusion(f32[2,16,16,128]{3,2,1,0:T(8,128)S(1)} %bitcast.13, f32[2,16,16,128]{3,2,1,0:T(8,128)S(1)} %bitcast.14, f32[2,16,16,128]{3,2,1,0:T(8,128)S(1)} %bitcast.15, f32[2,16,16,128]{3,2,1,0:T(8,128)S(1)} %bitcast.12), kind=kLoop, calls=%fused_computation | loop fusion | flops 786432 | bytes 2097152 | tf_op jit(solution)/shard_map/concatenate | solution.py:529
  (1 shorter events, 0.0 us)
